TPU v7x, 256 devices: a whole 4x4x8 slice. The times are simulated.
256 devices in a mesh: win: 4 (over z_lo, core), col: 64 (over z_hi, y, x).
Axes of the slice: x: 4, y: 4, z: 8 (z_hi: 4, z_lo: 2; z = z_hi * 2 + z_lo), core: 2. Of those that a mesh axis runs over, the one named last changes fastest.
Arguments:
- forcing: float32 [8, 256, 2, 192, 256], P('win', 'col'), may hold values from -6 to 6
- coefficients: bfloat16 [8, 256, 192, 512], P('win', 'col'), may hold values from -6 to 6
- legendre: float32 [256, 256, 256], P('col'), may hold values from -0.03125 to 0.03125
- weights: float32 [256], replicated, may hold values from 0.25 to 1
- damping: float32 [192, 256], replicated, may hold values from 0.3 to 1
- mixing: float32 [192, 192], replicated, may hold values from -0.4375 to 0.4375
- points: int32 [256], replicated, may hold values from 64 to 512, as said below
- wavenumbers: int32 [256], replicated, may hold values from 0 to 255, each once
Outputs:
- adjoint_output: float32 [8, 256, 2, 192, 256], P('win', 'col')
Inputs may be any that keep to these rules, and one draw needn't show every extreme that they name: 64 to 512 grid points on each latitude; the two latitudes next to the equator have 512. A permutation of the zonal wavenumbers 0 to 255; slot s of the spectral arrays holds wavenumber wavenumbers[s].
All inputs are finite; a program needn't handle non-finite values.
Results may differ from a plain program's by a relative error of at most 0.0003.
Values may be sent and summed in bfloat16 or wider, within the bound.
A program may use at most 128 MiB of HBM per device.

v0:
```python
import math

import jax
import jax.numpy as jnp
from jax import lax
from jax.sharding import PartitionSpec as P

STEPS = 2


HIGH = lax.Precision.HIGHEST


def passed_along(block, axis, distance):
    devices = range(lax.axis_size(axis))
    route = [(i - distance, i) for i in devices if i - distance in devices]
    return lax.ppermute(block, axis, route)


def fourier_table(count, slots, width):
    along = jnp.arange(width, dtype=jnp.int32)
    phase = slots[:, None] * along[None, :] % count
    angle = 2.0 * math.pi * phase.astype(jnp.float32) / count.astype(jnp.float32)
    live = (along < count).astype(jnp.float32)[None, :]
    return jnp.stack([jnp.cos(angle) * live, -jnp.sin(angle) * live], axis=1)


def shards(forcing, coefficients, legendre, weights, damping, mixing, points, wavenumbers):
    per_slot = legendre.shape[0]
    per_lat = coefficients.shape[1]
    levels = coefficients.shape[2]
    width = coefficients.shape[3]
    all_lat = legendre.shape[2]
    all_slots = wavenumbers.shape[0]
    column = lax.axis_index("col")
    own_slots = lax.dynamic_slice_in_dim(wavenumbers, column * per_slot, per_slot)
    degree = jnp.arange(legendre.shape[1], dtype=jnp.int32)
    masked = legendre * (degree[None, :, None] >= own_slots[:, None, None]).astype(jnp.float32)
    weighted = masked * weights[None, None, :]
    own_points = lax.dynamic_slice_in_dim(points, column * per_lat, per_lat)
    table = jax.vmap(fourier_table, (0, None, None))(own_points, wavenumbers, width)

    def adjoint_run(state, coef):
        batch = state.shape[0]
        for step in range(STEPS):
            four = jnp.einsum("snl,bsrfn->blsrf", masked, state, precision=HIGH)
            four = four.reshape(batch, all_lat, per_slot, 2 * levels)
            four = lax.all_to_all(four, "col", split_axis=1, concat_axis=2, tiled=True)
            four = four.reshape(batch, per_lat, all_slots, 2, levels)
            grid = jnp.einsum("blsrf,lsrj->blfj", four, table, precision=HIGH)
            forced = coef.astype(jnp.float32) * jnp.einsum(
                "blfj,fe->blej", grid, mixing, precision=HIGH
            )
            back = jnp.einsum("blfj,lsrj->blsrf", forced, table, precision=HIGH)
            back = back.reshape(batch, per_lat, all_slots, 2 * levels)
            back = lax.all_to_all(back, "col", split_axis=2, concat_axis=1, tiled=True)
            back = back.reshape(batch, all_lat, per_slot, 2, levels)
            state = damping * state + jnp.einsum("snl,blsrf->bsrfn", weighted, back, precision=HIGH)
        return state

    state_first = forcing[0]
    state_second = forcing[1]
    coef_first = coefficients[0]
    coef_second = coefficients[1]
    pairs = [(state_first, coef_first), (state_second, coef_second)]
    results = [adjoint_run(pair[0][None], pair[1][None])[0] for pair in pairs]
    arrived = passed_along(results[0], "win", -1)
    return jnp.stack([state_first - results[1], state_second - arrived])


def solution(mesh):
    in_specs = (
        P("win", "col", None, None, None),
        P("win", "col", None, None),
        P("col", None, None),
        P(),
        P(),
        P(),
        P(),
        P(),
    )
    out_specs = P("win", "col", None, None, None)
    return jax.shard_map(shards, mesh=mesh, in_specs=in_specs, out_specs=out_specs, check_vma=False)
```

profile of v0, /device:TPU:2, one launch (start us, length us, event | category | flops | bytes accessed | tf_op | source)
XLA Modules:
  0.0 414.0 jit_solution(17879088107324194257)
XLA Ops:
  0.9 3.4 fusion.48
  5.8 14.8 %all-to-all-start.4 = ((f32[1,256,4,384]{3,2,0,1:T(4,128)}), f32[1,256,4,384]{3,2,0,1:T(4,128)S(1)}, u32[]{:S(2)}, u32[]{:S(2)}) async-start(f32[1,256,4,384]{3,2,0,1:T(4,128)} %copy.63), calls=%async_computation.4 | async-start | bytes 3145728 | tf_op jit(solution)/shard_map/all_to_all | solution.py:48
  20.6 4.2 %fusion.53 = f32[4,256,2,192]{1,3,2,0:T(8,128)} fusion(f32[2,4,2,192,256]{4,3,2,1,0:T(8,128)} %param.8, f32[4,256,256]{2,1,0:T(8,128)S(1)} %copy-done.5, f32[4,256]{1,0:T(4,128)S(1)} %fusion.107), kind=kOutput, calls=%fused_computation.66 | convolution fusion | flops 1208221696 | bytes 4198400 | tf_op jit(solution)/shard_map/snl,bsrfn->blsrf/dot_general | solution.py:46
  27.4 33.4 %all-to-all-done.4 = f32[1,256,4,384]{3,2,0,1:T(4,128)S(1)} async-done(((f32[1,256,4,384]{3,2,0,1:T(4,128)}), f32[1,256,4,384]{3,2,0,1:T(4,128)S(1)}, u32[]{:S(2)}, u32[]{:S(2)}) %all-to-all-start.4) | async-done | bytes 1572896 | tf_op jit(solution)/shard_map/all_to_all | solution.py:48
  62.0 8.1 %all-to-all-start = ((f32[1,256,4,384]{3,2,0,1:T(4,128)}), f32[1,256,4,384]{3,2,0,1:T(4,128)}, u32[]{:S(2)}, u32[]{:S(2)}) async-start(f32[1,256,4,384]{3,2,0,1:T(4,128)} %copy.49), calls=%async_computation | async-start | bytes 3145728 | tf_op jit(solution)/shard_map/all_to_all | solution.py:48
  70.3 28.7 %cosine_multiply_fusion = (f32[4,256,1,512]{3,1,2,0:T(8,128)S(1)}, f32[4,256,1,512]{3,1,2,0:T(8,128)}) fusion(f32[4,512]{1,0:T(4,128)S(1)} %fusion.106, f32[4]{0:T(128)S(1)} %convert_element_type.41, pred[4]{0:T(512)(128)(4,1)S(1)} %broadcast_compare_fusion, s32[4]{0:T(128)S(1)} %get-tuple-element.5, s32[256,512]{1,0:T(8,128)S(1)} %iota_multiply_fusion), kind=kLoop, calls=%fused_computation.26 | loop fusion | flops 6815744 | bytes 4726820 | tf_op jit(solution)/shard_map/vmap()/mul | solution.py:25
  100.5 4.8 %reshape.253 = f32[4,256,2,192]{3,2,1,0:T(2,128)} reshape(f32[1,4,64,4,384]{4,3,2,1,0:T(4,128)} %copy.64) | data formatting | bytes 3145728 | tf_op jit(solution)/shard_map/reshape.47
  105.3 6.7 %fusion.9 = f32[4,512,192,1]{1,2,3,0:T(8,128)S(1)} fusion(f32[4,256,2,192]{3,2,1,0:T(2,128)} %reshape.253, f32[4,256,1,512]{3,1,2,0:T(8,128)} %get-tuple-element.8, f32[4,256,1,512]{3,1,2,0:T(8,128)S(1)} %get-tuple-element.7), kind=kOutput, calls=%fused_computation.15 | convolution fusion | flops 2416967680 | bytes 7340032 | tf_op jit(solution)/shard_map/blsrf,lsrj->blfj/dot_general | solution.py:50
  113.6 5.7 %fusion.28 = f32[4,256,2,192]{1,3,2,0:T(8,128)} fusion(f32[4,512,192]{1,2,0:T(8,128)S(1)} %fusion.37, bf16[2,4,192,512]{3,2,1,0:T(8,128)(2,1)S(1)} %copy-done.13, f32[4,256,1,512]{3,1,2,0:T(8,128)S(1)} %copy-done.1, f32[4,256,1,512]{3,1,2,0:T(8,128)S(1)} %get-tuple-element.7), kind=kOutput, calls=%fused_computation.38 | convolution fusion | flops 2417754112 | bytes 8126464 | tf_op jit(solution)/shard_map/blfj,lsrj->blsrf/dot_general | solution.py:54
  121.9 13.3 %all-to-all-start.5 = ((f32[1,4,256,384]{3,1,0,2:T(4,128)}), f32[1,4,256,384]{3,1,0,2:T(4,128)}, u32[]{:S(2)}, u32[]{:S(2)}) async-start(f32[1,4,256,384]{3,1,0,2:T(4,128)} %copy.67), calls=%async_computation.5 | async-start | bytes 3145728 | tf_op jit(solution)/shard_map/all_to_all | solution.py:56
  135.2 2.9 copy.50
  138.1 4.3 %reshape.241 = f32[4,256,2,192]{3,2,1,0:T(2,128)} reshape(f32[1,4,64,4,384]{4,3,2,1,0:T(4,128)} %copy.50) | data formatting | bytes 3145728 | tf_op jit(solution)/shard_map/reshape.7
  142.4 6.7 %fusion.17 = f32[4,512,192,1]{1,2,3,0:T(8,128)S(1)} fusion(f32[4,256,2,192]{3,2,1,0:T(2,128)} %reshape.241, f32[4,256,1,512]{3,1,2,0:T(8,128)} %get-tuple-element.8, f32[4,256,1,512]{3,1,2,0:T(8,128)S(1)} %get-tuple-element.7), kind=kOutput, calls=%fused_computation.23 | convolution fusion | flops 2416967680 | bytes 7340032 | tf_op jit(solution)/shard_map/blsrf,lsrj->blfj/dot_general | solution.py:50
  150.8 5.7 %fusion.22 = f32[4,256,2,192]{1,3,2,0:T(8,128)} fusion(f32[4,512,192]{1,2,0:T(8,128)S(1)} %fusion.43, bf16[2,4,192,512]{3,2,1,0:T(8,128)(2,1)S(1)} %copy-done.14, f32[4,256,1,512]{3,1,2,0:T(8,128)S(1)} %copy-done.2, f32[4,256,1,512]{3,1,2,0:T(8,128)S(1)} %get-tuple-element.7), kind=kOutput, calls=%fused_computation.34 | convolution fusion | flops 2417754112 | bytes 8126464 | tf_op jit(solution)/shard_map/blfj,lsrj->blsrf/dot_general | solution.py:54
  159.1 15.4 %all-to-all-done.5 = f32[1,4,256,384]{3,1,0,2:T(4,128)} async-done(((f32[1,4,256,384]{3,1,0,2:T(4,128)}), f32[1,4,256,384]{3,1,0,2:T(4,128)}, u32[]{:S(2)}, u32[]{:S(2)}) %all-to-all-start.5) | async-done | bytes 1572896 | tf_op jit(solution)/shard_map/all_to_all | solution.py:56
  174.5 8.0 %all-to-all-start.1 = ((f32[1,4,256,384]{3,1,0,2:T(4,128)}), f32[1,4,256,384]{3,1,0,2:T(4,128)}, u32[]{:S(2)}, u32[]{:S(2)}) async-start(f32[1,4,256,384]{3,1,0,2:T(4,128)} %copy.53), calls=%async_computation.1 | async-start | bytes 3145728 | tf_op jit(solution)/shard_map/all_to_all | solution.py:56
  182.5 3.0 copy.68
  185.5 4.3 %reshape.256 = f32[256,4,2,192]{3,2,1,0:T(2,128)} reshape(f32[1,64,4,4,384]{4,3,2,1,0:T(4,128)} %copy.68) | data formatting | bytes 3145728 | tf_op jit(solution)/shard_map/reshape.55
  189.8 6.0 %bitcast_add_fusion.1 = f32[1,4,2,192,256]{4,3,2,1,0:T(8,128)S(1)} fusion(f32[256,4,2,192]{3,2,1,0:T(2,128)} %reshape.256, f32[2,4,2,192,256]{4,3,2,1,0:T(8,128)} %param.8, f32[192,256]{1,0:T(8,128)S(1)} %copy-done.17, f32[4,256,256]{2,1,0:T(8,128)S(1)} %copy-done.5, f32[256]{0:T(256)S(1)} %copy-done.18, f32[4,256]{1,0:T(4,128)S(1)} %fusion.107), kind=kOutput, calls=%fused_computation.57 | convolution fusion | flops 1209270272 | bytes 5968896 | tf_op jit(solution)/shard_map/snl,blsrf->bsrfn/dot_general | solution.py:58
  195.8 2.9 fusion.46
  198.7 2.7 copy.70
  201.3 19.7 %all-to-all-done.1 = f32[1,4,256,384]{3,1,0,2:T(4,128)} async-done(((f32[1,4,256,384]{3,1,0,2:T(4,128)}), f32[1,4,256,384]{3,1,0,2:T(4,128)}, u32[]{:S(2)}, u32[]{:S(2)}) %all-to-all-start.1) | async-done | bytes 1572896 | tf_op jit(solution)/shard_map/all_to_all | solution.py:56
  221.1 9.8 %all-to-all-start.6 = ((f32[1,256,4,384]{3,2,0,1:T(4,128)}), f32[1,256,4,384]{3,2,0,1:T(4,128)}, u32[]{:S(2)}, u32[]{:S(2)}) async-start(f32[1,256,4,384]{3,2,0,1:T(4,128)} %copy.70), calls=%async_computation.6 | async-start | bytes 3145728 | tf_op jit(solution)/shard_map/all_to_all | solution.py:48
  230.9 3.0 copy.54
  233.9 4.3 %reshape.244 = f32[256,4,2,192]{3,2,1,0:T(2,128)} reshape(f32[1,64,4,4,384]{4,3,2,1,0:T(4,128)} %copy.54) | data formatting | bytes 3145728 | tf_op jit(solution)/shard_map/reshape.27
  238.2 6.0 %bitcast_add_fusion.3 = f32[1,4,2,192,256]{4,3,2,1,0:T(8,128)S(1)} fusion(f32[256,4,2,192]{3,2,1,0:T(2,128)} %reshape.244, f32[2,4,2,192,256]{4,3,2,1,0:T(8,128)} %param.8, f32[192,256]{1,0:T(8,128)S(1)} %copy-done.17, f32[4,256,256]{2,1,0:T(8,128)S(1)} %copy-done.5, f32[256]{0:T(256)S(1)} %copy-done.18, f32[4,256]{1,0:T(4,128)S(1)} %fusion.107), kind=kOutput, calls=%fused_computation.64 | convolution fusion | flops 1209270272 | bytes 5968896 | tf_op jit(solution)/shard_map/snl,blsrf->bsrfn/dot_general | solution.py:58
  244.2 2.9 fusion.51
  249.6 21.1 %all-to-all-done.6 = f32[1,256,4,384]{3,2,0,1:T(4,128)} async-done(((f32[1,256,4,384]{3,2,0,1:T(4,128)}), f32[1,256,4,384]{3,2,0,1:T(4,128)}, u32[]{:S(2)}, u32[]{:S(2)}) %all-to-all-start.6) | async-done | bytes 1572896 | tf_op jit(solution)/shard_map/all_to_all | solution.py:48
  270.7 7.8 %all-to-all-start.2 = ((f32[1,256,4,384]{3,2,0,1:T(4,128)}), f32[1,256,4,384]{3,2,0,1:T(4,128)}, u32[]{:S(2)}, u32[]{:S(2)}) async-start(f32[1,256,4,384]{3,2,0,1:T(4,128)} %copy.56), calls=%async_computation.2 | async-start | bytes 3145728 | tf_op jit(solution)/shard_map/all_to_all | solution.py:48
  278.5 2.8 copy.71
  281.3 4.3 %reshape.259 = f32[4,256,2,192]{3,2,1,0:T(2,128)} reshape(f32[1,4,64,4,384]{4,3,2,1,0:T(4,128)} %copy.71) | data formatting | bytes 3145728 | tf_op jit(solution)/shard_map/reshape.61
  285.6 6.7 %fusion.5 = f32[4,512,192,1]{1,2,3,0:T(8,128)S(1)} fusion(f32[4,256,2,192]{3,2,1,0:T(2,128)} %reshape.259, f32[4,256,1,512]{3,1,2,0:T(8,128)} %get-tuple-element.8, f32[4,256,1,512]{3,1,2,0:T(8,128)S(1)} %get-tuple-element.7), kind=kOutput, calls=%fused_computation.11 | convolution fusion | flops 2416967680 | bytes 7340032 | tf_op jit(solution)/shard_map/blsrf,lsrj->blfj/dot_general | solution.py:50
  294.0 5.7 %fusion.31 = f32[4,256,2,192]{1,3,2,0:T(8,128)} fusion(f32[4,512,192]{1,2,0:T(8,128)S(1)} %fusion.34, bf16[2,4,192,512]{3,2,1,0:T(8,128)(2,1)S(1)} %copy-done.15, f32[4,256,1,512]{3,1,2,0:T(8,128)S(1)} %copy-done.3, f32[4,256,1,512]{3,1,2,0:T(8,128)S(1)} %get-tuple-element.7), kind=kOutput, calls=%fused_computation.40 | convolution fusion | flops 2417754112 | bytes 8126464 | tf_op jit(solution)/shard_map/blfj,lsrj->blsrf/dot_general | solution.py:54
  302.2 12.6 %all-to-all-done.2 = f32[1,256,4,384]{3,2,0,1:T(4,128)} async-done(((f32[1,256,4,384]{3,2,0,1:T(4,128)}), f32[1,256,4,384]{3,2,0,1:T(4,128)}, u32[]{:S(2)}, u32[]{:S(2)}) %all-to-all-start.2) | async-done | bytes 1572896 | tf_op jit(solution)/shard_map/all_to_all | solution.py:48
  314.8 7.1 %all-to-all-start.7 = ((f32[1,4,256,384]{3,1,0,2:T(4,128)}), f32[1,4,256,384]{3,1,0,2:T(4,128)}, u32[]{:S(2)}, u32[]{:S(2)}) async-start(f32[1,4,256,384]{3,1,0,2:T(4,128)} %copy.74), calls=%async_computation.7 | async-start | bytes 3145728 | tf_op jit(solution)/shard_map/all_to_all | solution.py:56
  321.9 2.8 copy.57
  324.7 4.3 %reshape.247 = f32[4,256,2,192]{3,2,1,0:T(2,128)} reshape(f32[1,4,64,4,384]{4,3,2,1,0:T(4,128)} %copy.57) | data formatting | bytes 3145728 | tf_op jit(solution)/shard_map/reshape.33
  329.0 6.7 %fusion.13 = f32[4,512,192,1]{1,2,3,0:T(8,128)S(1)} fusion(f32[4,256,2,192]{3,2,1,0:T(2,128)} %reshape.247, f32[4,256,1,512]{3,1,2,0:T(8,128)} %get-tuple-element.8, f32[4,256,1,512]{3,1,2,0:T(8,128)S(1)} %get-tuple-element.7), kind=kOutput, calls=%fused_computation.19 | convolution fusion | flops 2416967680 | bytes 7340032 | tf_op jit(solution)/shard_map/blsrf,lsrj->blfj/dot_general | solution.py:50
  337.4 5.7 %fusion.25 = f32[4,256,2,192]{1,3,2,0:T(8,128)} fusion(f32[4,512,192]{1,2,0:T(8,128)S(1)} %fusion.40, bf16[2,4,192,512]{3,2,1,0:T(8,128)(2,1)S(1)} %copy-done.16, f32[4,256,1,512]{3,1,2,0:T(8,128)S(1)} %copy-done.4, f32[4,256,1,512]{3,1,2,0:T(8,128)S(1)} %get-tuple-element.7), kind=kOutput, calls=%fused_computation.36 | convolution fusion | flops 2417754112 | bytes 8126464 | tf_op jit(solution)/shard_map/blfj,lsrj->blsrf/dot_general | solution.py:54
  345.7 14.2 %all-to-all-done.7 = f32[1,4,256,384]{3,1,0,2:T(4,128)} async-done(((f32[1,4,256,384]{3,1,0,2:T(4,128)}), f32[1,4,256,384]{3,1,0,2:T(4,128)}, u32[]{:S(2)}, u32[]{:S(2)}) %all-to-all-start.7) | async-done | bytes 1572896 | tf_op jit(solution)/shard_map/all_to_all | solution.py:56
  360.0 7.6 %all-to-all-start.3 = ((f32[1,4,256,384]{3,1,0,2:T(4,128)}), f32[1,4,256,384]{3,1,0,2:T(4,128)}, u32[]{:S(2)}, u32[]{:S(2)}) async-start(f32[1,4,256,384]{3,1,0,2:T(4,128)} %copy.60), calls=%async_computation.3 | async-start | bytes 3145728 | tf_op jit(solution)/shard_map/all_to_all | solution.py:56
  367.6 3.0 copy.75
  370.6 4.4 %reshape.262 = f32[256,4,2,192]{3,2,1,0:T(2,128)} reshape(f32[1,64,4,4,384]{4,3,2,1,0:T(4,128)} %copy.75) | data formatting | bytes 3145728 | tf_op jit(solution)/shard_map/reshape.69
  375.0 6.7 %fusion.45 = f32[4,2,192,256]{3,2,1,0:T(8,128)} fusion(f32[1,4,2,192,256]{4,3,2,1,0:T(8,128)S(1)} %copy-done.8, f32[256,4,2,192]{3,2,1,0:T(2,128)} %reshape.262, f32[192,256]{1,0:T(8,128)S(1)} %copy-done.17, f32[4,256,256]{2,1,0:T(8,128)S(1)} %copy-done.5, f32[256]{0:T(256)S(1)} %copy-done.18, f32[4,256]{1,0:T(4,128)S(1)} %fusion.107), kind=kOutput, calls=%fused_computation.54 | convolution fusion | flops 1209270272 | bytes 5968896 | tf_op jit(solution)/shard_map/snl,blsrf->bsrfn/dot_general | solution.py:58
  383.1 13.5 %all-to-all-done.3 = f32[1,4,256,384]{3,1,0,2:T(4,128)} async-done(((f32[1,4,256,384]{3,1,0,2:T(4,128)}), f32[1,4,256,384]{3,1,0,2:T(4,128)}, u32[]{:S(2)}, u32[]{:S(2)}) %all-to-all-start.3) | async-done | bytes 1572896 | tf_op jit(solution)/shard_map/all_to_all | solution.py:56
  396.6 3.1 copy.61
  399.6 4.4 %reshape.250 = f32[256,4,2,192]{3,2,1,0:T(2,128)} reshape(f32[1,64,4,4,384]{4,3,2,1,0:T(4,128)} %copy.61) | data formatting | bytes 3145728 | tf_op jit(solution)/shard_map/reshape.41
  404.0 6.2 %fusion.50 = f32[1,4,2,192,256]{4,3,2,1,0:T(8,128)S(1)} fusion(f32[1,4,2,192,256]{4,3,2,1,0:T(8,128)S(1)} %copy-done.10, f32[256,4,2,192]{3,2,1,0:T(2,128)} %reshape.250, f32[2,4,2,192,256]{4,3,2,1,0:T(8,128)} %param.8, f32[192,256]{1,0:T(8,128)S(1)} %copy-done.17, f32[4,256,256]{2,1,0:T(8,128)S(1)} %copy-done.5, f32[256]{0:T(256)S(1)} %copy-done.18, ...), kind=kOutput, calls=%fused_computation.61 | convolution fusion | flops 1209663488 | bytes 7541760 | tf_op jit(solution)/shard_map/snl,blsrf->bsrfn/dot_general | solution.py:58
  (66 shorter events, 32.3 us)
Async XLA Ops:
  0.0 112.0 %copy-start = (f32[192,192]{1,0:T(8,128)S(1)}, f32[192,192]{1,0:T(8,128)}, u32[]{:S(2)}) copy-start(f32[192,192]{1,0:T(8,128)} %param.13) | copy-start | bytes 442372
  5.8 14.8 %copy-start.5 = (f32[4,256,256]{2,1,0:T(8,128)S(1)}, f32[4,256,256]{2,1,0:T(8,128)}, u32[]{:S(2)}) copy-start(f32[4,256,256]{2,1,0:T(8,128)} %param.10) | copy-start | bytes 3145732
  5.8 55.0 %all-to-all-start.4 = ((f32[1,256,4,384]{3,2,0,1:T(4,128)}), f32[1,256,4,384]{3,2,0,1:T(4,128)S(1)}, u32[]{:S(2)}, u32[]{:S(2)}) async-start(f32[1,256,4,384]{3,2,0,1:T(4,128)} %copy.63), calls=%async_computation.4 | async-start | bytes 3145728 | tf_op jit(solution)/shard_map/all_to_all | solution.py:48
  27.4 42.6 %copy-start.20 = (s32[256]{0:T(256)S(1)}, s32[256]{0:T(256)}, u32[]{:S(2)}) copy-start(s32[256]{0:T(256)} %param.14) | copy-start | bytes 3076
  27.4 42.8 %copy-start.19 = (s32[256]{0:T(256)S(1)}, s32[256]{0:T(256)}, u32[]{:S(2)}) copy-start(s32[256]{0:T(256)} %param.15) | copy-start | bytes 3076
  60.8 1.1 copy-start.11
  62.0 60.0 %all-to-all-start = ((f32[1,256,4,384]{3,2,0,1:T(4,128)}), f32[1,256,4,384]{3,2,0,1:T(4,128)}, u32[]{:S(2)}, u32[]{:S(2)}) async-start(f32[1,256,4,384]{3,2,0,1:T(4,128)} %copy.49), calls=%async_computation | async-start | bytes 3145728 | tf_op jit(solution)/shard_map/all_to_all | solution.py:48
  70.3 28.7 %copy-start.12 = (f32[1,256,4,384]{3,2,0,1:T(4,128)S(1)}, f32[1,256,4,384]{3,2,0,1:T(4,128)}, u32[]{:S(2)}) copy-start(f32[1,256,4,384]{3,2,0,1:T(4,128)} %copy-done.11) | copy-start | bytes 4718596
  105.3 8.4 %copy-start.13 = (bf16[2,4,192,512]{3,2,1,0:T(8,128)(2,1)S(1)}, bf16[2,4,192,512]{3,2,1,0:T(8,128)(2,1)}, u32[]{:S(2)}) copy-start(bf16[2,4,192,512]{3,2,1,0:T(8,128)(2,1)} %param.9) | copy-start | bytes 4718596
  112.0 1.7 copy-start.1
  121.9 52.5 %all-to-all-start.5 = ((f32[1,4,256,384]{3,1,0,2:T(4,128)}), f32[1,4,256,384]{3,1,0,2:T(4,128)}, u32[]{:S(2)}, u32[]{:S(2)}) async-start(f32[1,4,256,384]{3,1,0,2:T(4,128)} %copy.67), calls=%async_computation.5 | async-start | bytes 3145728 | tf_op jit(solution)/shard_map/all_to_all | solution.py:56
  142.4 8.3 %copy-start.14 = (bf16[2,4,192,512]{3,2,1,0:T(8,128)(2,1)S(1)}, bf16[2,4,192,512]{3,2,1,0:T(8,128)(2,1)}, u32[]{:S(2)}) copy-start(bf16[2,4,192,512]{3,2,1,0:T(8,128)(2,1)} %param.9) | copy-start | bytes 4718596
  149.1 1.7 copy-start.2
  174.5 46.6 %all-to-all-start.1 = ((f32[1,4,256,384]{3,1,0,2:T(4,128)}), f32[1,4,256,384]{3,1,0,2:T(4,128)}, u32[]{:S(2)}, u32[]{:S(2)}) async-start(f32[1,4,256,384]{3,1,0,2:T(4,128)} %copy.53), calls=%async_computation.1 | async-start | bytes 3145728 | tf_op jit(solution)/shard_map/all_to_all | solution.py:56
  185.5 4.3 %copy-start.17 = (f32[192,256]{1,0:T(8,128)S(1)}, f32[192,256]{1,0:T(8,128)}, u32[]{:S(2)}) copy-start(f32[192,256]{1,0:T(8,128)} %param.12) | copy-start | bytes 589828
  185.5 4.3 %copy-start.18 = (f32[256]{0:T(256)S(1)}, f32[256]{0:T(256)}, u32[]{:S(2)}) copy-start(f32[256]{0:T(256)} %param.11) | copy-start | bytes 3076
  195.8 2.9 copy-start.7
  221.1 49.6 %all-to-all-start.6 = ((f32[1,256,4,384]{3,2,0,1:T(4,128)}), f32[1,256,4,384]{3,2,0,1:T(4,128)}, u32[]{:S(2)}, u32[]{:S(2)}) async-start(f32[1,256,4,384]{3,2,0,1:T(4,128)} %copy.70), calls=%async_computation.6 | async-start | bytes 3145728 | tf_op jit(solution)/shard_map/all_to_all | solution.py:48
  244.2 2.9 copy-start.9
  270.7 44.2 %all-to-all-start.2 = ((f32[1,256,4,384]{3,2,0,1:T(4,128)}), f32[1,256,4,384]{3,2,0,1:T(4,128)}, u32[]{:S(2)}, u32[]{:S(2)}) async-start(f32[1,256,4,384]{3,2,0,1:T(4,128)} %copy.56), calls=%async_computation.2 | async-start | bytes 3145728 | tf_op jit(solution)/shard_map/all_to_all | solution.py:48
  285.6 8.3 %copy-start.15 = (bf16[2,4,192,512]{3,2,1,0:T(8,128)(2,1)S(1)}, bf16[2,4,192,512]{3,2,1,0:T(8,128)(2,1)}, u32[]{:S(2)}) copy-start(bf16[2,4,192,512]{3,2,1,0:T(8,128)(2,1)} %param.9) | copy-start | bytes 4718596
  292.3 1.7 copy-start.3
  314.8 45.1 %all-to-all-start.7 = ((f32[1,4,256,384]{3,1,0,2:T(4,128)}), f32[1,4,256,384]{3,1,0,2:T(4,128)}, u32[]{:S(2)}, u32[]{:S(2)}) async-start(f32[1,4,256,384]{3,1,0,2:T(4,128)} %copy.74), calls=%async_computation.7 | async-start | bytes 3145728 | tf_op jit(solution)/shard_map/all_to_all | solution.py:56
  329.0 8.3 %copy-start.16 = (bf16[2,4,192,512]{3,2,1,0:T(8,128)(2,1)S(1)}, bf16[2,4,192,512]{3,2,1,0:T(8,128)(2,1)}, u32[]{:S(2)}) copy-start(bf16[2,4,192,512]{3,2,1,0:T(8,128)(2,1)} %param.9) | copy-start | bytes 4718596
  335.7 1.7 copy-start.4
  360.0 36.6 %all-to-all-start.3 = ((f32[1,4,256,384]{3,1,0,2:T(4,128)}), f32[1,4,256,384]{3,1,0,2:T(4,128)}, u32[]{:S(2)}, u32[]{:S(2)}) async-start(f32[1,4,256,384]{3,1,0,2:T(4,128)} %copy.60), calls=%async_computation.3 | async-start | bytes 3145728 | tf_op jit(solution)/shard_map/all_to_all | solution.py:56
  370.6 4.4 %copy-start.8 = (f32[1,4,2,192,256]{4,3,2,1,0:T(8,128)S(1)}, f32[1,4,2,192,256]{4,3,2,1,0:T(8,128)}, u32[]{:S(2)}) copy-start(f32[1,4,2,192,256]{4,3,2,1,0:T(8,128)} %copy-done.7) | copy-start | bytes 4718596
  381.7 28.6 %collective-permute-start = (f32[4,2,192,256]{3,2,1,0:T(8,128)}, f32[4,2,192,256]{3,2,1,0:T(8,128)}, u32[]{:S(2)}, u32[]{:S(2)}) collective-permute-start(f32[4,2,192,256]{3,2,1,0:T(8,128)} %fusion.45), channel_id=1, source_target_pairs={{64,0},{128,64},{192,128},{65,1},{129,65},{193,129},{66,2},{130,66... | collective-permute-start | bytes 4718600 | tf_op jit(solution)/shard_map/ppermute | solution.py:17
  399.6 4.4 %copy-start.10 = (f32[1,4,2,192,256]{4,3,2,1,0:T(8,128)S(1)}, f32[1,4,2,192,256]{4,3,2,1,0:T(8,128)}, u32[]{:S(2)}) copy-start(f32[1,4,2,192,256]{4,3,2,1,0:T(8,128)} %copy-done.9) | copy-start | bytes 4718596
  404.0 6.2 %copy-start.6 = (f32[2,4,2,192,256]{4,3,2,1,0:T(8,128)S(1)}, f32[2,4,2,192,256]{4,3,2,1,0:T(8,128)}, u32[]{:S(2)}) copy-start(f32[2,4,2,192,256]{4,3,2,1,0:T(8,128)} %param.8) | copy-start | bytes 9437188
where the time goes:
time: 420 us; the launch traced here: 414 us
  waiting for transfers between devices  130 us (31%)
  matrix products  94.2 us (22%)
  local copies, waits for them, and re-layouts  78.8 us (19%)
  starting transfers between devices  77.9 us (19%)
  other arithmetic  32.6 us (8%)
    all_to_all x4, waiting for transfers between devices, adjoint_run(): four = lax.all_to_all(four, 'col', split_axis=1, concat_axis=2, tiled=True)  67.1 us
    all_to_all x4, waiting for transfers between devices, adjoint_run(): back = lax.all_to_all(back, 'col', split_axis=2, concat_axis=1, tiled=True)  62.8 us
    all_to_all x4, starting transfers between devices, adjoint_run(): four = lax.all_to_all(four, 'col', split_axis=1, concat_axis=2, tiled=True)  40.5 us
    all_to_all x4, starting transfers between devices, adjoint_run(): back = lax.all_to_all(back, 'col', split_axis=2, concat_axis=1, tiled=True)  36 us
    another operation x8, local copies, waits for them, and re-layouts  35.1 us
    mul x1, other arithmetic, fourier_table(): return jnp.stack([jnp.cos(angle) * live, -jnp.sin(angle) * live], axis=1)  28.7 us
    dot_general x4, matrix products, adjoint_run(): grid = jnp.einsum('blsrf,lsrj->blfj', four, table, precision=HIGH)  26.7 us
    dot_general x4, matrix products, adjoint_run(): jnp.einsum('snl,blsrf->bsrfn', weighted, back, precision=HIGH)  24.8 us
  transfers between devices with their start and end apart: 9, of which 7 were waited for; matrix products, arithmetic and copies ran while one was open for 47% of the time, Pallas kernels for 0%

commit v1 on v0

v1 whole, which is shorter than its diff:
```python
import functools
import math

import jax
import jax.numpy as jnp
from jax import lax
from jax.experimental import pallas as pl
from jax.experimental.pallas import tpu as pltpu
from jax.sharding import PartitionSpec as P

STEPS = 2
SLOTS = 4
COLS = 64
ROWS = 16
LEVELS = 192
SIZE = 256
WIDTH = 512
LANES = 384
PARTS = 3
TOP = 32767.0

f32 = jnp.float32
bf16 = jnp.bfloat16
MESH = pl.DeviceIdType.MESH


def split(values):
    high = values.astype(bf16)
    return high, (values - high.astype(f32)).astype(bf16)


def dot(a, b):
    return lax.dot_general(a, b, (((1,), (0,)), ((), ())), preferred_element_type=f32)


def dot_t(a, b):
    return lax.dot_general(a, b, (((1,), (1,)), ((), ())), preferred_element_type=f32)


def dot3(a_high, a_low, b_high, b_low, product=dot):
    return product(a_high, b_high) + (product(a_high, b_low) + product(a_low, b_high))


def widened(row):
    return jnp.concatenate([row] * PARTS, axis=1)


def kernel(
    forcing, coefs, legendre, weights, damping, mixing, row_numbers, points, numbers,
    out,
    send, recv, send_scale, recv_scale, passed, passed_scale,
    stage, state, fwd_high, fwd_low, inv_high, inv_low, damp, mix_pad, mix_high, mix_low,
    perm, eye, tab_high, tab_low, tabt_high, tabt_low, coef_t, op_high, op_low,
    send_sem, recv_sem, send_scale_sem, recv_scale_sem, pass_sem,
):
    win = lax.axis_index("win")
    col = lax.axis_index("col")
    at_z, at_y, at_x = col // 16, (col // 4) % 4, col % 4

    def partner(k):
        z = (at_z + k // 16) % 4
        y = (at_y + (k // 4) % 4) % 4
        x = (at_x + k % 4) % 4
        return z * 16 + y * 4 + x

    barrier = pltpu.get_barrier_semaphore()

    def greet(k, carry):
        pl.semaphore_signal(barrier, inc=1, device_id=(win, partner(k)), device_id_type=MESH)
        return carry

    lax.fori_loop(1, COLS, greet, 0)

    @pl.when(win > 0)
    def _():
        pl.semaphore_signal(barrier, inc=1, device_id=(win - 1, col), device_id_type=MESH)

    @pl.when(win < 3)
    def _():
        pl.semaphore_signal(barrier, inc=1, device_id=(win + 1, col), device_id_type=MESH)

    def in_order(x):
        return jnp.concatenate([x[0, :128], x[1, :128], x[0, 128:], x[1, 128:]], axis=0)

    def spread(values, row, rows):
        for part in range(PARTS):
            stage[part, pl.ds(row, rows, stride=ROWS), :] = values[:, part * 128:(part + 1) * 128]

    def gathered(row, part):
        return stage[part, pl.ds(row, COLS, stride=ROWS), :]

    def peak(values):
        top = jnp.max(jnp.abs(values), axis=0, keepdims=True)
        return jnp.maximum(jnp.maximum(top[:, :128], top[:, 128:256]), top[:, 256:384])

    def encode(top, buf):
        top = jnp.maximum(top, 1e-30)
        send_scale[buf] = top * (1.0 / TOP)
        inverse = TOP / top

        def one(d, carry):
            for part in range(PARTS):
                code = jnp.round(stage[part, pl.ds(pl.multiple_of(d * ROWS, ROWS), ROWS), :] * inverse)
                send[buf, d, :, part * 128:(part + 1) * 128] = code.astype(jnp.int32).astype(jnp.int16)
            return carry

        lax.fori_loop(0, COLS, one, 0, unroll=4)

    def decode(codes, scales):
        def one(d, carry):
            scale = scales(d)
            for part in range(PARTS):
                code = codes(d, part).astype(jnp.int32).astype(f32)
                stage[part, pl.ds(pl.multiple_of(d * ROWS, ROWS), ROWS), :] = code * scale
            return carry

        lax.fori_loop(0, COLS, one, 0, unroll=4)

    def start(buf):
        def one(k, carry):
            d = partner(k)
            pltpu.make_async_remote_copy(
                src_ref=send_scale.at[buf], dst_ref=recv_scale.at[buf, col],
                send_sem=send_scale_sem.at[buf], recv_sem=recv_scale_sem.at[buf],
                device_id=(win, d), device_id_type=MESH,
            ).start()
            pltpu.make_async_remote_copy(
                src_ref=send.at[buf, d], dst_ref=recv.at[buf, col],
                send_sem=send_sem.at[buf], recv_sem=recv_sem.at[buf],
                device_id=(win, d), device_id_type=MESH,
            ).start()
            return carry

        lax.fori_loop(1, COLS, one, 0)
        recv[buf, col] = send[buf, col]
        recv_scale[buf, col] = send_scale[buf]

    def wait_for(buf, data_sem, scale_sem):
        some = recv.at[buf, pl.ds(0, COLS - 1)]
        pltpu.make_async_copy(some, some, data_sem.at[buf]).wait()
        some = recv_scale.at[buf, pl.ds(0, COLS - 1)]
        pltpu.make_async_copy(some, some, scale_sem.at[buf]).wait()

    def arrive(buf):
        wait_for(buf, recv_sem, recv_scale_sem)
        decode(
            lambda d, part: recv[buf, d, :, part * 128:(part + 1) * 128],
            lambda d: recv_scale[buf, d],
        )

    def sent(buf):
        wait_for(buf, send_sem, send_scale_sem)

    def live(sub):
        return jnp.logical_or(sub > 0, win > 0)

    row = lax.broadcasted_iota(jnp.int32, (SIZE, SIZE), 0)
    lane = lax.broadcasted_iota(jnp.int32, (SIZE, SIZE), 1)
    perm[...] = (row == 4 * (lane % COLS) + lane // COLS).astype(f32).astype(bf16)
    eye[...] = (row == lane).astype(f32).astype(bf16)
    permt = (lane == 4 * (row % COLS) + row // COLS).astype(f32).astype(bf16)

    def masked(s):
        keep = (row >= numbers[col * SLOTS + s]).astype(f32)
        return legendre[s] * keep

    def forward_table(s, carry):
        high, low = split(masked(s))
        fwd_high[s] = dot_t(permt, high).astype(bf16)
        fwd_low[s] = dot_t(permt, low).astype(bf16)
        return carry

    lax.fori_loop(0, SLOTS, forward_table, 0)

    def first(sub, carry):
        @pl.when(live(sub))
        def _():
            def slot(s, top):
                high, low = split(in_order(forcing[sub, s]))
                four = dot3(fwd_high[s], fwd_low[s], high, low, dot_t)
                for q in range(SLOTS):
                    spread(four[q * COLS:(q + 1) * COLS], q * SLOTS + s, COLS)
                return jnp.maximum(top, peak(four))

            encode(lax.fori_loop(0, SLOTS, slot, jnp.zeros((1, 128), f32)), sub)

            @pl.when(sub == jnp.where(win > 0, 0, 1))
            def _():
                pl.semaphore_wait(barrier, COLS - 1 + jnp.where(win > 0, 1, 0) + jnp.where(win < 3, 1, 0))

            start(sub)

        return carry

    lax.fori_loop(0, 2, first, 0)

    def inverse_table(s, carry):
        high, low = split(masked(s) * weights[...])
        inv_high[s] = dot(high, perm[...]).astype(bf16)
        inv_low[s] = dot(low, perm[...]).astype(bf16)
        return carry

    lax.fori_loop(0, SLOTS, inverse_table, 0)

    mix_pad[...] = jnp.zeros((SIZE, SIZE), f32)
    mix_pad[:LEVELS, :LEVELS] = mixing[...]
    high, low = split(mix_pad[...])
    mix_high[...] = high
    mix_low[...] = low

    damp_t = jnp.transpose(jnp.concatenate([damping[...], damping[128:]], axis=0))
    damp[...] = jnp.concatenate([damp_t[:, :128], damp_t[:, :128], damp_t[:, 128:]], axis=1)

    wave = jnp.broadcast_to(row_numbers[...].astype(f32).astype(bf16), (16, SIZE))
    wave = dot(wave, perm[...])[:1]

    def table(q, carry):
        count = points[col * SLOTS + q]
        count_f = jnp.full((1, SIZE), count, jnp.int32).astype(f32)
        part_of = 1.0 / count_f

        def angles(rows, step):
            j = (step * lax.broadcasted_iota(jnp.int32, (rows, SIZE), 0)).astype(f32)
            product = j * wave
            rest = product - jnp.floor(product * part_of) * count_f
            rest = jnp.where(rest < 0.0, rest + count_f, rest)
            rest = jnp.where(rest >= count_f, rest - count_f, rest)
            angle = (2.0 * math.pi) * rest / count_f
            return jnp.cos(angle), jnp.sin(angle)

        cos_a, sin_a = angles(WIDTH // 16, 16)
        cos_b, sin_b = angles(16, 1)
        near = lax.broadcasted_iota(jnp.int32, (16, SIZE), 0)
        for a in range(WIDTH // 16):
            keep = (near + 16 * a < count).astype(f32)
            ca, sa = cos_a[a:a + 1] , sin_a[a:a + 1]
            cos = (ca * cos_b - sa * sin_b) * keep
            sin = (sa * cos_b + ca * sin_b) * keep
            for r, value in ((0, cos), (1, -sin)):
                high, low = split(value)
                tabt_high[q, a * 16:(a + 1) * 16, r * SIZE:(r + 1) * SIZE] = high
                tabt_low[q, a * 16:(a + 1) * 16, r * SIZE:(r + 1) * SIZE] = low
        for r in range(2):
            cut = slice(r * SIZE, (r + 1) * SIZE)
            tab_high[q, cut, :] = dot_t(eye[...], tabt_high[q, :, cut]).astype(bf16)
            tab_low[q, cut, :] = dot_t(eye[...], tabt_low[q, :, cut]).astype(bf16)
        for sub in range(2):
            padded = jnp.concatenate([coefs[sub, q], jnp.zeros((SIZE - LEVELS, WIDTH), bf16)], axis=0)
            for h in range(2):
                cut = slice(h * SIZE, (h + 1) * SIZE)
                coef_t[sub, q, cut, :] = dot_t(eye[...], padded[:, cut]).astype(bf16)
        return carry

    lax.fori_loop(0, SLOTS, table, 0)

    def grid(sub, step):
        arrive(sub)
        if step > 0:
            sent(2 + sub)

        def latitude(q, carry):
            for s in range(SLOTS):
                at = q * SLOTS + s
                last = gathered(at, 2)
                real = jnp.concatenate([gathered(at, 0), last], axis=1)
                imag = jnp.concatenate([gathered(at, 1), pltpu.roll(last, 64, 1)], axis=1)
                for r, value in ((0, real), (1, imag)):
                    high, low = split(value)
                    rows = slice(r * SIZE + s * COLS, r * SIZE + (s + 1) * COLS)
                    op_high[q, rows, :] = high
                    op_low[q, rows, :] = low
            return carry

        lax.fori_loop(0, SLOTS, latitude, 0)

        def latitude(q, top):
            values = dot3(tabt_high[q], tabt_low[q], op_high[q], op_low[q])
            high, low = split(values)
            mixed = dot3(high, low, mix_high[...], mix_low[...])
            high, low = split(mixed * coef_t[sub, q].astype(f32))
            back = dot3(tab_high[q], tab_low[q], high, low)
            for s in range(SLOTS):
                real = back[s * COLS:(s + 1) * COLS]
                imag = back[SIZE + s * COLS:SIZE + (s + 1) * COLS]
                last = real[:, 128:] + pltpu.roll(imag[:, 128:], 64, 1)
                values = jnp.concatenate([real[:, :128], imag[:, :128], last], axis=1)
                spread(values, q * SLOTS + s, COLS)
                top = jnp.maximum(top, peak(values))
            return top

        encode(lax.fori_loop(0, SLOTS, latitude, jnp.zeros((1, 128), f32)), 2 + sub)
        start(2 + sub)

    def spectral(sub, step):
        arrive(2 + sub)
        sent(sub)
        last = step == STEPS - 1

        def operands(s, carry):
            for q in range(SLOTS):
                values = jnp.concatenate([gathered(q * SLOTS + s, part) for part in range(PARTS)], axis=1)
                high, low = split(values)
                rows = slice(q * COLS, (q + 1) * COLS)
                for half, value in ((op_high, high), (op_low, low)):
                    half[s, rows, :] = value[:, :SIZE]
                    half[s, SIZE + q * COLS:SIZE + (q + 1) * COLS, :128] = value[:, SIZE:]
            return carry

        lax.fori_loop(0, SLOTS, operands, 0)

        def slot(s, top):
            cut = slice(SIZE, 2 * SIZE)
            inc = jnp.concatenate([
                dot3(inv_high[s], inv_low[s], op_high[s, :SIZE], op_low[s, :SIZE]),
                dot3(inv_high[s], inv_low[s], op_high[s, cut, :128], op_low[s, cut, :128]),
            ], axis=1)
            if step == 0:
                before = jnp.transpose(in_order(forcing[sub, s]))
            else:
                before = state[sub, s]
            after = damp[...] * before + inc
            if not last:
                state[sub, s] = after
                high, low = split(after)
                four = dot3(fwd_high[s], fwd_low[s], high, low)
                for q in range(SLOTS):
                    spread(four[q * COLS:(q + 1) * COLS], q * SLOTS + s, COLS)
                return jnp.maximum(top, peak(four))
            state[sub, s] = after
            return jnp.maximum(top, peak(after))

        top = lax.fori_loop(0, SLOTS, slot, jnp.zeros((1, 128), f32))
        if not last:
            encode(top, sub)
            start(sub)
        else:
            sent(2 + sub)

            @pl.when(sub == 0)
            def _():
                for s in range(SLOTS):
                    for part in range(PARTS):
                        stage[part, s * SIZE:(s + 1) * SIZE, :] = state[0, s, :, part * 128:(part + 1) * 128]
                encode(top, 0)
                pltpu.make_async_remote_copy(
                    src_ref=send_scale.at[0], dst_ref=passed_scale,
                    send_sem=pass_sem.at[0], recv_sem=pass_sem.at[1],
                    device_id=(win - 1, col), device_id_type=MESH,
                ).start()
                pltpu.make_async_remote_copy(
                    src_ref=send.at[0], dst_ref=passed,
                    send_sem=pass_sem.at[2], recv_sem=pass_sem.at[3],
                    device_id=(win - 1, col), device_id_type=MESH,
                ).start()

    for step in range(STEPS):
        for phase in (grid, spectral):
            def both(sub, carry):
                @pl.when(live(sub))
                def _():
                    phase(sub, step)

                return carry

            lax.fori_loop(0, 2, both, 0)

    def write(index, s, result):
        flat = jnp.transpose(result)
        for r in range(2):
            out[index, s, r, :128] = forcing[index, s, r, :128] - flat[r * 128:(r + 1) * 128]
            out[index, s, r, 128:] = forcing[index, s, r, 128:] - flat[256 + r * 64:256 + (r + 1) * 64]

    def near_result(s, carry):
        write(0, s, state[1, s])
        return carry

    lax.fori_loop(0, SLOTS, near_result, 0)

    @pl.when(win > 0)
    def _():
        pltpu.make_async_copy(send_scale.at[0], send_scale.at[0], pass_sem.at[0]).wait()
        pltpu.make_async_copy(send.at[0], send.at[0], pass_sem.at[2]).wait()

    @pl.when(win < 3)
    def _():
        pltpu.make_async_copy(passed_scale, passed_scale, pass_sem.at[1]).wait()
        pltpu.make_async_copy(passed, passed, pass_sem.at[3]).wait()
        decode(
            lambda d, part: passed[d, :, part * 128:(part + 1) * 128],
            lambda d: passed_scale[...],
        )

        def far_result(s, carry):
            rows = pl.ds(pl.multiple_of(s * SIZE, SIZE), SIZE)
            write(1, s, jnp.concatenate([stage[part, rows, :] for part in range(PARTS)], axis=1))
            return carry

        lax.fori_loop(0, SLOTS, far_result, 0)

    @pl.when(win == 3)
    def _():
        def own(s, carry):
            out[1, s] = forcing[1, s]
            return carry

        lax.fori_loop(0, SLOTS, own, 0)


def shards(forcing, coefficients, legendre, weights, damping, mixing, points, wavenumbers):
    vmem = pl.BlockSpec(memory_space=pltpu.VMEM)
    smem = pl.BlockSpec(memory_space=pltpu.SMEM)
    dma = pltpu.SemaphoreType.DMA
    return pl.pallas_call(
        kernel,
        out_shape=jax.ShapeDtypeStruct(forcing.shape, f32),
        in_specs=[vmem] * 7 + [smem] * 2,
        out_specs=vmem,
        scratch_shapes=[
            pltpu.VMEM((4, COLS, ROWS, LANES), jnp.int16),
            pltpu.VMEM((4, COLS, ROWS, LANES), jnp.int16),
            pltpu.VMEM((4, 1, 128), f32),
            pltpu.VMEM((4, COLS, 1, 128), f32),
            pltpu.VMEM((COLS, ROWS, LANES), jnp.int16),
            pltpu.VMEM((1, 128), f32),
            pltpu.VMEM((PARTS, COLS * ROWS, 128), f32),
            pltpu.VMEM((2, SLOTS, SIZE, LANES), f32),
            pltpu.VMEM((SLOTS, SIZE, SIZE), bf16),
            pltpu.VMEM((SLOTS, SIZE, SIZE), bf16),
            pltpu.VMEM((SLOTS, SIZE, SIZE), bf16),
            pltpu.VMEM((SLOTS, SIZE, SIZE), bf16),
            pltpu.VMEM((SIZE, LANES), f32),
            pltpu.VMEM((SIZE, SIZE), f32),
            pltpu.VMEM((SIZE, SIZE), bf16),
            pltpu.VMEM((SIZE, SIZE), bf16),
            pltpu.VMEM((SIZE, SIZE), bf16),
            pltpu.VMEM((SIZE, SIZE), bf16),
            pltpu.VMEM((SLOTS, WIDTH, WIDTH), bf16),
            pltpu.VMEM((SLOTS, WIDTH, WIDTH), bf16),
            pltpu.VMEM((SLOTS, WIDTH, WIDTH), bf16),
            pltpu.VMEM((SLOTS, WIDTH, WIDTH), bf16),
            pltpu.VMEM((2, SLOTS, WIDTH, SIZE), bf16),
            pltpu.VMEM((SLOTS, WIDTH, SIZE), bf16),
            pltpu.VMEM((SLOTS, WIDTH, SIZE), bf16),
            dma((4,)), dma((4,)), dma((4,)), dma((4,)), dma((4,)),
        ],
        compiler_params=pltpu.CompilerParams(
            collective_id=0, has_side_effects=True, vmem_limit_bytes=56 * 2**20
        ),
        name="adjoint",
    )(
        forcing, coefficients, legendre, weights.reshape(1, SIZE), damping, mixing,
        wavenumbers.reshape(1, SIZE), points, wavenumbers,
    )


def solution(mesh):
    in_specs = (
        P("win", "col", None, None, None),
        P("win", "col", None, None),
        P("col", None, None),
        P(),
        P(),
        P(),
        P(),
        P(),
    )
    out_specs = P("win", "col", None, None, None)
    return jax.shard_map(shards, mesh=mesh, in_specs=in_specs, out_specs=out_specs, check_vma=False)
```

time: 420 us -> 196 us (0.47)
  the two profiles are of different devices: /device:TPU:2 before, /device:TPU:1 now
where the time goes in v1:
time: 196 us; the launch traced here: 195 us
  Pallas kernels  192 us (98%)
  local copies, waits for them, and re-layouts  3.83 us (2%)
    pallas_call x1, Pallas kernels, shards(): pl.pallas_call(kernel, out_shape=jax.ShapeDtypeStruct(forcing.shape, f32)...  192 us

profile of v1, /device:TPU:1, one launch (start us, length us, event | category | flops | bytes accessed | tf_op | source)
XLA Modules:
  0.0 195.4 jit_solution(7915665306703045115)
XLA Ops:
  0.0 191.6 %adjoint.1 = f32[2,4,2,192,256]{4,3,2,1,0:T(8,128)} custom-call(f32[2,4,2,192,256]{4,3,2,1,0:T(8,128)} %forcing.1, bf16[2,4,192,512]{3,2,1,0:T(8,128)(2,1)} %coefs.1, f32[4,256,256]{2,1,0:T(8,128)} %legendre.1, f32[1,256]{1,0:T(1,128)} %bitcast.3, f32[192,256]{1,0:T(8,128)} %damping.1, f32[192,192]{1,0:T(8,128)} %mixing.1, s32[1,256]{1,0:T(1,128)} %bitcast.2, ...), custom_call_target="tpu_custom_call" | custom-call | tf_op jit(solution)/shard_map/adjoint/pallas_call | solution.py:413
  191.6 3.8 %copy.10 = f32[2,4,2,192,256]{4,3,2,1,0:T(8,128)} copy(f32[2,4,2,192,256]{4,3,2,1,0:T(8,128)} %adjoint.1) | data formatting | bytes 6291456

commit v2 on v1

--- a/solution.py
+++ b/solution.py
@@ -17,6 +17,8 @@
 WIDTH = 512
 LANES = 384
 PARTS = 3
+RELAYED = 8
+GROUP = 8
 TOP = 32767.0
 
 f32 = jnp.float32
@@ -48,14 +50,17 @@
 def kernel(
     forcing, coefs, legendre, weights, damping, mixing, row_numbers, points, numbers,
     out,
-    send, recv, send_scale, recv_scale, passed, passed_scale,
+    send, recv, send_scale, recv_scale, relay, passed, passed_scale,
     stage, state, fwd_high, fwd_low, inv_high, inv_low, damp, mix_pad, mix_high, mix_low,
     perm, eye, tab_high, tab_low, tabt_high, tabt_low, coef_t, op_high, op_low,
-    send_sem, recv_sem, send_scale_sem, recv_scale_sem, pass_sem,
+    send_sem, recv_sem, relay_sem, forward_sem,
+    near_send_sem, near_recv_sem, far_send_sem, far_recv_sem, pass_sem,
 ):
     win = lax.axis_index("win")
     col = lax.axis_index("col")
     at_z, at_y, at_x = col // 16, (col // 4) % 4, col % 4
+    group, member = col // GROUP, col % GROUP
+    lighter = jnp.where(win < 2, 3, 1)
 
     def partner(k):
         z = (at_z + k // 16) % 4
@@ -116,40 +121,101 @@
 
         lax.fori_loop(0, COLS, one, 0, unroll=4)
 
+    def copy_to(target, src, dst, send_by, recv_by):
+        pltpu.make_async_remote_copy(
+            src_ref=src, dst_ref=dst, send_sem=send_by, recv_sem=recv_by,
+            device_id=(win, target), device_id_type=MESH,
+        ).start()
+
+    def wait_blocks(count, sem):
+        some = recv.at[0, pl.ds(0, count)]
+        pltpu.make_async_copy(some, some, sem).wait()
+
+    def wait_scales(count, sem):
+        some = recv_scale.at[0, pl.ds(0, count)]
+        pltpu.make_async_copy(some, some, sem).wait()
+
     def start(buf):
-        def one(k, carry):
-            d = partner(k)
-            pltpu.make_async_remote_copy(
-                src_ref=send_scale.at[buf], dst_ref=recv_scale.at[buf, col],
-                send_sem=send_scale_sem.at[buf], recv_sem=recv_scale_sem.at[buf],
-                device_id=(win, d), device_id_type=MESH,
-            ).start()
-            pltpu.make_async_remote_copy(
-                src_ref=send.at[buf, d], dst_ref=recv.at[buf, col],
-                send_sem=send_sem.at[buf], recv_sem=recv_sem.at[buf],
-                device_id=(win, d), device_id_type=MESH,
-            ).start()
-            return carry
-
-        lax.fori_loop(1, COLS, one, 0)
+        def block(target):
+            copy_to(target, send.at[buf, target], recv.at[buf, col], send_sem.at[buf], recv_sem.at[buf])
+
+        def scale(k, carry):
+            target = group * GROUP + (member + k) % GROUP
+            copy_to(target, send_scale.at[buf], recv_scale.at[buf, col], near_send_sem.at[buf], near_recv_sem.at[buf])
+            return carry
+
+        def opposite(k, carry):
+            block(((at_z + 2) % 4) * 16 + (2 + (at_y + k // 4) % 2) * 4 + (at_x + k) % 4)
+            return carry
+
+        def beside(k, carry):
+            place = ((at_y + k // 4) % 4) * 4 + (at_x + k) % 4
+            block(((at_z + 1) % 4) * 16 + place)
+            block(((at_z + 3) % 4) * 16 + place)
+            return carry
+
+        def level(k, carry):
+            block(at_z * 16 + ((at_y + k // 4) % 4) * 4 + (at_x + k) % 4)
+            return carry
+
+        recv_scale[buf, col] = send_scale[buf]
+        lax.fori_loop(1, GROUP, scale, 0)
+        copy_to(
+            ((at_z + lighter) % 4) * 16 + at_y * 4 + at_x,
+            send.at[buf, pl.ds(((at_z + 2) % 4) * 16, RELAYED)], relay.at[buf], send_sem.at[buf], relay_sem.at[buf],
+        )
+        lax.fori_loop(0, RELAYED, opposite, 0)
+        lax.fori_loop(0, 16, beside, 0)
+        lax.fori_loop(1, 16, level, 0)
         recv[buf, col] = send[buf, col]
-        recv_scale[buf, col] = send_scale[buf]
-
-    def wait_for(buf, data_sem, scale_sem):
-        some = recv.at[buf, pl.ds(0, COLS - 1)]
-        pltpu.make_async_copy(some, some, data_sem.at[buf]).wait()
-        some = recv_scale.at[buf, pl.ds(0, COLS - 1)]
-        pltpu.make_async_copy(some, some, scale_sem.at[buf]).wait()
-
-    def arrive(buf):
-        wait_for(buf, recv_sem, recv_scale_sem)
+
+    def forward(buf):
+        wait_blocks(RELAYED, relay_sem.at[buf])
+        source = ((at_z + 4 - lighter) % 4) * 16 + at_y * 4 + at_x
+
+        def block(k, carry):
+            place = ((at_y + k // 4) % 2) * 4 + (at_x + k) % 4
+            copy_to(
+                ((at_z + lighter) % 4) * 16 + place,
+                relay.at[buf, place], recv.at[buf, source], forward_sem.at[buf], recv_sem.at[buf],
+            )
+            return carry
+
+        lax.fori_loop(0, RELAYED, block, 0)
+        wait_scales(GROUP - 1, near_recv_sem.at[buf])
+
+        def scales(k, carry):
+            some = recv_scale.at[buf, pl.ds(group * GROUP, GROUP)]
+            copy_to(((group + k) % GROUP) * GROUP + member, some, some, far_send_sem.at[buf], far_recv_sem.at[buf])
+            return carry
+
+        lax.fori_loop(1, GROUP, scales, 0)
+
+    def settle(buf):
+        wait_blocks(RELAYED, forward_sem.at[buf])
+        wait_scales((GROUP - 1) * GROUP, far_send_sem.at[buf])
+
+    def sent(buf):
+        wait_blocks(COLS - 1, send_sem.at[buf])
+        wait_scales(GROUP - 1, near_send_sem.at[buf])
+
+    def arrive(buf, other, more=True):
+        wait_blocks(COLS - 1, recv_sem.at[buf])
+        wait_scales((GROUP - 1) * GROUP, far_recv_sem.at[buf])
+
+        @pl.when(jnp.logical_and(win > 0, more))
+        def _():
+            forward(other)
+
         decode(
             lambda d, part: recv[buf, d, :, part * 128:(part + 1) * 128],
             lambda d: recv_scale[buf, d],
         )
 
-    def sent(buf):
-        wait_for(buf, send_sem, send_scale_sem)
+    def follow(sub, buf):
+        @pl.when(win == 0)
+        def _():
+            forward(buf)
 
     def live(sub):
         return jnp.logical_or(sub > 0, win > 0)
@@ -188,7 +254,12 @@
             def _():
                 pl.semaphore_wait(barrier, COLS - 1 + jnp.where(win > 0, 1, 0) + jnp.where(win < 3, 1, 0))
 
+            @pl.when(jnp.logical_and(win > 0, sub == 1))
+            def _():
+                forward(0)
+
             start(sub)
+            follow(sub, sub)
 
         return carry
 
@@ -254,7 +325,7 @@
     lax.fori_loop(0, SLOTS, table, 0)
 
     def grid(sub, step):
-        arrive(sub)
+        arrive(sub, jnp.where(sub == 0, 1, 2))
         if step > 0:
             sent(2 + sub)
 
@@ -289,12 +360,14 @@
             return top
 
         encode(lax.fori_loop(0, SLOTS, latitude, jnp.zeros((1, 128), f32)), 2 + sub)
+        settle(sub)
         start(2 + sub)
+        follow(sub, 2 + sub)
 
     def spectral(sub, step):
-        arrive(2 + sub)
+        last = step == STEPS - 1
+        arrive(2 + sub, jnp.where(sub == 0, 3, 0), jnp.logical_or(not last, sub == 0))
         sent(sub)
-        last = step == STEPS - 1
 
         def operands(s, carry):
             for q in range(SLOTS):
@@ -332,9 +405,12 @@
         top = lax.fori_loop(0, SLOTS, slot, jnp.zeros((1, 128), f32))
         if not last:
             encode(top, sub)
+            settle(2 + sub)
             start(sub)
+            follow(sub, sub)
         else:
             sent(2 + sub)
+            settle(2 + sub)
 
             @pl.when(sub == 0)
             def _():
@@ -420,6 +496,7 @@
             pltpu.VMEM((4, COLS, ROWS, LANES), jnp.int16),
             pltpu.VMEM((4, 1, 128), f32),
             pltpu.VMEM((4, COLS, 1, 128), f32),
+            pltpu.VMEM((4, RELAYED, ROWS, LANES), jnp.int16),
             pltpu.VMEM((COLS, ROWS, LANES), jnp.int16),
             pltpu.VMEM((1, 128), f32),
             pltpu.VMEM((PARTS, COLS * ROWS, 128), f32),
@@ -441,6 +518,7 @@
             pltpu.VMEM((2, SLOTS, WIDTH, SIZE), bf16),
             pltpu.VMEM((SLOTS, WIDTH, SIZE), bf16),
             pltpu.VMEM((SLOTS, WIDTH, SIZE), bf16),
+            dma((4,)), dma((4,)), dma((4,)), dma((4,)),
             dma((4,)), dma((4,)), dma((4,)), dma((4,)), dma((4,)),
         ],
         compiler_params=pltpu.CompilerParams(

time: 196 us -> 167 us (0.85)
  Pallas kernels: 192 us -> 163 us
    pallas_call x1, Pallas kernels: 192 us -> 163 us  [shards(): pl.pallas_call(kernel, out_shape=jax.ShapeDtypeStruct(forcing.shape, f32)...]
where the time goes in v2:
time: 167 us
  Pallas kernels  163 us (98%)
  local copies, waits for them, and re-layouts  3.83 us (2%)
    pallas_call x1, Pallas kernels, shards(): pl.pallas_call(kernel, out_shape=jax.ShapeDtypeStruct(forcing.shape, f32)...  163 us
    unnamed x1, local copies, waits for them, and re-layouts  3.83 us

profile of v2, /device:TPU:1, one launch (start us, length us, event | category | flops | bytes accessed | tf_op | source)
XLA Modules:
  0.0 166.8 jit_solution(2315586173277944908)
XLA Ops:
  0.0 163.0 %adjoint.1 = f32[2,4,2,192,256]{4,3,2,1,0:T(8,128)} custom-call(f32[2,4,2,192,256]{4,3,2,1,0:T(8,128)} %forcing.1, bf16[2,4,192,512]{3,2,1,0:T(8,128)(2,1)} %coefs.1, f32[4,256,256]{2,1,0:T(8,128)} %legendre.1, f32[1,256]{1,0:T(1,128)} %bitcast.3, f32[192,256]{1,0:T(8,128)} %damping.1, f32[192,192]{1,0:T(8,128)} %mixing.1, s32[1,256]{1,0:T(1,128)} %bitcast.2, ...), custom_call_target="tpu_custom_call" | custom-call | tf_op jit(solution)/shard_map/adjoint/pallas_call | solution.py:489
  163.0 3.8 %copy.10 = f32[2,4,2,192,256]{4,3,2,1,0:T(8,128)} copy(f32[2,4,2,192,256]{4,3,2,1,0:T(8,128)} %adjoint.1) | data formatting | bytes 6291456

commit v3 on v2

--- a/solution.py
+++ b/solution.py
@@ -19,6 +19,7 @@
 PARTS = 3
 RELAYED = 8
 GROUP = 8
+UNROLL = 4
 TOP = 32767.0
 
 f32 = jnp.float32
@@ -43,18 +44,15 @@
     return product(a_high, b_high) + (product(a_high, b_low) + product(a_low, b_high))
 
 
-def widened(row):
-    return jnp.concatenate([row] * PARTS, axis=1)
-
-
 def kernel(
-    forcing, coefs, legendre, weights, damping, mixing, row_numbers, points, numbers,
-    out,
+    forcing_in, coefs_in, legendre_in, weights, damping, mixing, row_numbers, points, numbers,
+    out_in,
+    forcing, coefs, legendre, out,
     send, recv, send_scale, recv_scale, relay, passed, passed_scale,
     stage, state, fwd_high, fwd_low, inv_high, inv_low, damp, mix_pad, mix_high, mix_low,
     perm, eye, tab_high, tab_low, tabt_high, tabt_low, coef_t, op_high, op_low,
     send_sem, recv_sem, relay_sem, forward_sem,
-    near_send_sem, near_recv_sem, far_send_sem, far_recv_sem, pass_sem,
+    near_send_sem, near_recv_sem, far_send_sem, far_recv_sem, pass_sem, load_sem, store_sem,
 ):
     win = lax.axis_index("win")
     col = lax.axis_index("col")
@@ -67,6 +65,15 @@
         y = (at_y + (k // 4) % 4) % 4
         x = (at_x + k % 4) % 4
         return z * 16 + y * 4 + x
+
+    loads = [
+        pltpu.make_async_copy(legendre_in, legendre, load_sem.at[2]),
+        pltpu.make_async_copy(forcing_in.at[0], forcing.at[0], load_sem.at[0]),
+        pltpu.make_async_copy(forcing_in.at[1], forcing.at[1], load_sem.at[1]),
+        pltpu.make_async_copy(coefs_in, coefs, load_sem.at[3]),
+    ]
+    for load in loads:
+        load.start()
 
     barrier = pltpu.get_barrier_semaphore()
 
@@ -236,9 +243,12 @@
         fwd_low[s] = dot_t(permt, low).astype(bf16)
         return carry
 
-    lax.fori_loop(0, SLOTS, forward_table, 0)
+    loads[0].wait()
+    lax.fori_loop(0, SLOTS, forward_table, 0, unroll=UNROLL)
 
     def first(sub, carry):
+        pltpu.make_async_copy(forcing_in.at[sub], forcing.at[sub], load_sem.at[sub]).wait()
+
         @pl.when(live(sub))
         def _():
             def slot(s, top):
@@ -248,7 +258,7 @@
                     spread(four[q * COLS:(q + 1) * COLS], q * SLOTS + s, COLS)
                 return jnp.maximum(top, peak(four))
 
-            encode(lax.fori_loop(0, SLOTS, slot, jnp.zeros((1, 128), f32)), sub)
+            encode(lax.fori_loop(0, SLOTS, slot, jnp.zeros((1, 128), f32), unroll=UNROLL), sub)
 
             @pl.when(sub == jnp.where(win > 0, 0, 1))
             def _():
@@ -271,7 +281,7 @@
         inv_low[s] = dot(low, perm[...]).astype(bf16)
         return carry
 
-    lax.fori_loop(0, SLOTS, inverse_table, 0)
+    lax.fori_loop(0, SLOTS, inverse_table, 0, unroll=UNROLL)
 
     mix_pad[...] = jnp.zeros((SIZE, SIZE), f32)
     mix_pad[:LEVELS, :LEVELS] = mixing[...]
@@ -322,7 +332,36 @@
                 coef_t[sub, q, cut, :] = dot_t(eye[...], padded[:, cut]).astype(bf16)
         return carry
 
+    loads[3].wait()
     lax.fori_loop(0, SLOTS, table, 0)
+
+    def write(index, s, result):
+        flat = jnp.transpose(result)
+        for r in range(2):
+            out[index, s, r, :128] = forcing[index, s, r, :128] - flat[r * 128:(r + 1) * 128]
+            out[index, s, r, 128:] = forcing[index, s, r, 128:] - flat[256 + r * 64:256 + (r + 1) * 64]
+        pltpu.make_async_copy(out.at[index, s], out_in.at[index, s], store_sem.at[index]).start()
+
+    def far_results():
+        @pl.when(win < 3)
+        def _():
+            pltpu.make_async_copy(passed_scale, passed_scale, pass_sem.at[1]).wait()
+            pltpu.make_async_copy(passed, passed, pass_sem.at[3]).wait()
+            decode(
+                lambda d, part: passed[d, :, part * 128:(part + 1) * 128],
+                lambda d: passed_scale[...],
+            )
+
+            def far_result(s, carry):
+                rows = pl.ds(pl.multiple_of(s * SIZE, SIZE), SIZE)
+                write(1, s, jnp.concatenate([stage[part, rows, :] for part in range(PARTS)], axis=1))
+                return carry
+
+            lax.fori_loop(0, SLOTS, far_result, 0)
+
+        @pl.when(win == 3)
+        def _():
+            pltpu.make_async_copy(forcing.at[1], out_in.at[1], store_sem.at[1]).start()
 
     def grid(sub, step):
         arrive(sub, jnp.where(sub == 0, 1, 2))
@@ -342,7 +381,7 @@
                     op_low[q, rows, :] = low
             return carry
 
-        lax.fori_loop(0, SLOTS, latitude, 0)
+        lax.fori_loop(0, SLOTS, latitude, 0, unroll=UNROLL)
 
         def latitude(q, top):
             values = dot3(tabt_high[q], tabt_low[q], op_high[q], op_low[q])
@@ -359,13 +398,18 @@
                 top = jnp.maximum(top, peak(values))
             return top
 
-        encode(lax.fori_loop(0, SLOTS, latitude, jnp.zeros((1, 128), f32)), 2 + sub)
+        encode(lax.fori_loop(0, SLOTS, latitude, jnp.zeros((1, 128), f32), unroll=UNROLL), 2 + sub)
         settle(sub)
         start(2 + sub)
         follow(sub, 2 + sub)
 
     def spectral(sub, step):
         last = step == STEPS - 1
+        if last:
+            @pl.when(sub == 1)
+            def _():
+                far_results()
+
         arrive(2 + sub, jnp.where(sub == 0, 3, 0), jnp.logical_or(not last, sub == 0))
         sent(sub)
 
@@ -379,7 +423,7 @@
                     half[s, SIZE + q * COLS:SIZE + (q + 1) * COLS, :128] = value[:, SIZE:]
             return carry
 
-        lax.fori_loop(0, SLOTS, operands, 0)
+        lax.fori_loop(0, SLOTS, operands, 0, unroll=UNROLL)
 
         def slot(s, top):
             cut = slice(SIZE, 2 * SIZE)
@@ -402,7 +446,7 @@
             state[sub, s] = after
             return jnp.maximum(top, peak(after))
 
-        top = lax.fori_loop(0, SLOTS, slot, jnp.zeros((1, 128), f32))
+        top = lax.fori_loop(0, SLOTS, slot, jnp.zeros((1, 128), f32), unroll=UNROLL)
         if not last:
             encode(top, sub)
             settle(2 + sub)
@@ -440,12 +484,6 @@
 
             lax.fori_loop(0, 2, both, 0)
 
-    def write(index, s, result):
-        flat = jnp.transpose(result)
-        for r in range(2):
-            out[index, s, r, :128] = forcing[index, s, r, :128] - flat[r * 128:(r + 1) * 128]
-            out[index, s, r, 128:] = forcing[index, s, r, 128:] - flat[256 + r * 64:256 + (r + 1) * 64]
-
     def near_result(s, carry):
         write(0, s, state[1, s])
         return carry
@@ -457,29 +495,8 @@
         pltpu.make_async_copy(send_scale.at[0], send_scale.at[0], pass_sem.at[0]).wait()
         pltpu.make_async_copy(send.at[0], send.at[0], pass_sem.at[2]).wait()
 
-    @pl.when(win < 3)
-    def _():
-        pltpu.make_async_copy(passed_scale, passed_scale, pass_sem.at[1]).wait()
-        pltpu.make_async_copy(passed, passed, pass_sem.at[3]).wait()
-        decode(
-            lambda d, part: passed[d, :, part * 128:(part + 1) * 128],
-            lambda d: passed_scale[...],
-        )
-
-        def far_result(s, carry):
-            rows = pl.ds(pl.multiple_of(s * SIZE, SIZE), SIZE)
-            write(1, s, jnp.concatenate([stage[part, rows, :] for part in range(PARTS)], axis=1))
-            return carry
-
-        lax.fori_loop(0, SLOTS, far_result, 0)
-
-    @pl.when(win == 3)
-    def _():
-        def own(s, carry):
-            out[1, s] = forcing[1, s]
-            return carry
-
-        lax.fori_loop(0, SLOTS, own, 0)
+    for index in range(2):
+        pltpu.make_async_copy(out.at[index], out_in.at[index], store_sem.at[index]).wait()
 
 
 def shards(forcing, coefficients, legendre, weights, damping, mixing, points, wavenumbers):
@@ -489,9 +506,13 @@
     return pl.pallas_call(
         kernel,
         out_shape=jax.ShapeDtypeStruct(forcing.shape, f32),
-        in_specs=[vmem] * 7 + [smem] * 2,
-        out_specs=vmem,
+        in_specs=[pl.BlockSpec(memory_space=pl.ANY)] * 3 + [vmem] * 4 + [smem] * 2,
+        out_specs=pl.BlockSpec(memory_space=pl.ANY),
         scratch_shapes=[
+            pltpu.VMEM(forcing.shape, f32),
+            pltpu.VMEM(coefficients.shape, bf16),
+            pltpu.VMEM(legendre.shape, f32),
+            pltpu.VMEM(forcing.shape, f32),
             pltpu.VMEM((4, COLS, ROWS, LANES), jnp.int16),
             pltpu.VMEM((4, COLS, ROWS, LANES), jnp.int16),
             pltpu.VMEM((4, 1, 128), f32),
@@ -519,7 +540,7 @@
             pltpu.VMEM((SLOTS, WIDTH, SIZE), bf16),
             pltpu.VMEM((SLOTS, WIDTH, SIZE), bf16),
             dma((4,)), dma((4,)), dma((4,)), dma((4,)),
-            dma((4,)), dma((4,)), dma((4,)), dma((4,)), dma((4,)),
+            dma((4,)), dma((4,)), dma((4,)), dma((4,)), dma((4,)), dma((4,)), dma((2,)),
         ],
         compiler_params=pltpu.CompilerParams(
             collective_id=0, has_side_effects=True, vmem_limit_bytes=56 * 2**20

time: 167 us -> 163 us (0.976)
  Pallas kernels: 163 us -> 159 us
    pallas_call x1, Pallas kernels: 163 us -> 159 us  [shards(): pl.pallas_call(kernel, out_shape=jax.ShapeDtypeStruct(forcing.shape, f32)...]
where the time goes in v3:
time: 163 us
  Pallas kernels  159 us (98%)
  local copies, waits for them, and re-layouts  3.83 us (2%)
    pallas_call x1, Pallas kernels, shards(): pl.pallas_call(kernel, out_shape=jax.ShapeDtypeStruct(forcing.shape, f32)...  159 us
    unnamed x1, local copies, waits for them, and re-layouts  3.83 us

profile of v3, /device:TPU:1, one launch (start us, length us, event | category | flops | bytes accessed | tf_op | source)
XLA Modules:
  0.0 162.8 jit_solution(1489329811232190033)
XLA Ops:
  0.0 158.9 %adjoint.1 = f32[2,4,2,192,256]{4,3,2,1,0:T(8,128)} custom-call(f32[2,4,2,192,256]{4,3,2,1,0:T(8,128)} %forcing_in.1, bf16[2,4,192,512]{3,2,1,0:T(8,128)(2,1)} %coefs_in.1, f32[4,256,256]{2,1,0:T(8,128)} %legendre_in.1, f32[1,256]{1,0:T(1,128)} %bitcast.3, f32[192,256]{1,0:T(8,128)} %damping.1, f32[192,192]{1,0:T(8,128)} %mixing.1, s32[1,256]{1,0:T(1,128)} %bitcast.2, ...), custom_call_target="tpu_custom_call" | custom-call | tf_op jit(solution)/shard_map/adjoint/pallas_call | solution.py:506
  158.9 3.8 %copy.10 = f32[2,4,2,192,256]{4,3,2,1,0:T(8,128)} copy(f32[2,4,2,192,256]{4,3,2,1,0:T(8,128)} %adjoint.1) | data formatting | bytes 6291456
